TPU v7x, 128 devices: a whole 4x4x4 slice. The times are simulated.
128 devices in a mesh: dp: 16 (over z, x_hi, core), ctx: 8 (over x_lo, y).
Axes of the slice: x: 4 (x_hi: 2, x_lo: 2; x = x_hi * 2 + x_lo), y: 4, z: 4, core: 2. Of those that a mesh axis runs over, the one named last changes fastest.
Arguments:
- queries: bfloat16 [16, 1024, 2048], P('dp', 'ctx'), may hold values from -5 to 5
- keys: bfloat16 [16, 1024, 2048], P('dp', 'ctx'), may hold values from -5 to 5
- values: bfloat16 [16, 1024, 2048], P('dp', 'ctx'), may hold values from -12 to 12
- out_weight: bfloat16 [2048, 2048], P(('dp', 'ctx')), may hold values from -0.5 to 0.5
- cotangent: bfloat16 [16, 1024, 2048], P('dp', 'ctx'), may hold values from -6 to 6
- rand_blocks: int32 [16, 16, 16, 3], P('dp', 'ctx'), may hold values from 0 to 15
- glob_blocks: int32 [16, 2], P('dp'), may hold values from 0 to 15
Outputs:
- mixed: bfloat16 [16, 1024, 2048], P('dp', 'ctx')
- grad_queries: bfloat16 [16, 1024, 2048], P('dp', 'ctx')
- grad_keys: bfloat16 [16, 1024, 2048], P('dp', 'ctx')
- grad_values: bfloat16 [16, 1024, 2048], P('dp', 'ctx')
- grad_weight: float32 [2048, 2048], P(('dp', 'ctx'))
Inputs may be any that keep to these rules, and one draw needn't show every extreme that they name: `glob_blocks`: each entry names a block of the document.
All inputs are finite; a program needn't handle non-finite values.
Results may differ from a plain program's by a relative error of at most 0.015.
Values may be sent and summed in bfloat16 or wider, within the bound.
No kernel may reach another device: no remote copies, remote signals or barrier semaphores. Data moves between devices by JAX's collectives and lax.ppermute only.
A program may use at most 128 MiB of HBM per device.

v0:
```python
import math
import jax
import jax.numpy as jnp
from jax import lax
from jax.sharding import PartitionSpec as P

HS = 128
BLK = 64
WIN = 1
masked_score = -1e30


def block_lists(rand_rows, glob_row, block_count):
    head_count = rand_rows.shape[0]
    width = 2 * WIN + 1
    offsets = jnp.arange(-WIN, WIN + 1, dtype=jnp.int32)
    window = jnp.arange(block_count, dtype=jnp.int32)[:, None] + offsets[None, :]
    inside = (window >= 0) & (window < block_count)
    window = jnp.clip(window, 0, block_count - 1)
    lists = jnp.concatenate(
        [
            jnp.broadcast_to(window, (head_count, block_count, width)),
            jnp.broadcast_to(glob_row[None, None, :], (head_count, block_count, glob_row.shape[0])),
            rand_rows,
        ],
        axis=-1,
    )
    in_range = jnp.concatenate(
        [
            jnp.broadcast_to(inside, (head_count, block_count, width)),
            jnp.ones((head_count, block_count, lists.shape[-1] - width), dtype=jnp.bool_),
        ],
        axis=-1,
    )
    positions = jnp.arange(lists.shape[-1], dtype=jnp.int32)
    earlier = positions[None, :] < positions[:, None]
    matching = lists[..., :, None] == lists[..., None, :]
    repeated = jnp.any(matching & earlier & in_range[..., None, :], axis=-1)
    return (lists, in_range & jnp.logical_not(repeated))


def head_pass(query_blocks, key_blocks, value_blocks, cot_blocks, lists, live_entries):
    scale = 1.0 / math.sqrt(HS)
    key_sets = key_blocks[lists]
    value_sets = value_blocks[lists]
    live_mask = live_entries[:, None, :, None]
    scores = (
        jnp.einsum("nqd,nekd->nqek", query_blocks, key_sets, preferred_element_type=jnp.float32)
        * scale
    )
    scores = jnp.where(live_mask, scores, masked_score)
    row_max = jnp.max(scores, axis=(2, 3), keepdims=True)
    unnormed = jnp.where(live_mask, jnp.exp(scores - row_max), 0.0)
    probs = unnormed / jnp.sum(unnormed, axis=(2, 3), keepdims=True)
    probs_low = probs.astype(jnp.bfloat16)
    attended = jnp.einsum(
        "nqek,nekd->nqd", probs_low, value_sets, preferred_element_type=jnp.float32
    ).astype(jnp.bfloat16)
    delta = jnp.sum(cot_blocks.astype(jnp.float32) * attended.astype(jnp.float32), axis=-1)
    prob_grad = jnp.einsum(
        "nqd,nekd->nqek", cot_blocks, value_sets, preferred_element_type=jnp.float32
    )
    score_grad = (probs * (prob_grad - delta[:, :, None, None])).astype(jnp.bfloat16)
    query_grad = (
        jnp.einsum("nqek,nekd->nqd", score_grad, key_sets, preferred_element_type=jnp.float32)
        * scale
    )
    key_terms = (
        jnp.einsum("nqek,nqd->nekd", score_grad, query_blocks, preferred_element_type=jnp.float32)
        * scale
    )
    value_terms = jnp.einsum(
        "nqek,nqd->nekd", probs_low, cot_blocks, preferred_element_type=jnp.float32
    )
    flat_lists = lists.reshape(-1)
    block_count = key_blocks.shape[0]
    key_grad = jax.ops.segment_sum(
        key_terms.reshape(flat_lists.shape[0], -1), flat_lists, num_segments=block_count
    )
    value_grad = jax.ops.segment_sum(
        value_terms.reshape(flat_lists.shape[0], -1), flat_lists, num_segments=block_count
    )
    return (
        attended,
        query_grad.astype(jnp.bfloat16),
        key_grad.reshape(key_blocks.shape).astype(jnp.bfloat16),
        value_grad.reshape(value_blocks.shape).astype(jnp.bfloat16),
    )


def on_device(queries, keys, values, out_weight, cotangent, rand_blocks, glob_blocks):
    cot_rows = cotangent[0]
    full_weight = lax.all_gather(out_weight, ("dp", "ctx"), axis=0, tiled=True)
    head_cot = jnp.dot(cot_rows, full_weight, preferred_element_type=jnp.float32)
    head_cot = head_cot.astype(jnp.bfloat16)[None]
    query_heads, key_heads, value_heads, cot_heads = (
        lax.all_to_all(queries, "ctx", split_axis=2, concat_axis=1, tiled=True),
        lax.all_to_all(keys, "ctx", split_axis=2, concat_axis=1, tiled=True),
        lax.all_to_all(values, "ctx", split_axis=2, concat_axis=1, tiled=True),
        lax.all_to_all(head_cot, "ctx", split_axis=2, concat_axis=1, tiled=True),
    )
    head_count = rand_blocks.shape[1]
    block_count = rand_blocks.shape[2]
    group_len = query_heads.shape[1]

    def split(heads_layout):
        return heads_layout[0].reshape(block_count, BLK, head_count, HS).transpose(2, 0, 1, 3)

    def join(blocks):
        return blocks.transpose(1, 2, 0, 3).reshape(1, group_len, head_count * HS)

    lists, live_entries = block_lists(rand_blocks[0], glob_blocks[0], block_count)

    def per_head(parts):
        return head_pass(*parts)

    attended, query_grad, key_grad, value_grad = lax.map(
        per_head,
        (
            split(query_heads),
            split(key_heads),
            split(value_heads),
            split(cot_heads),
            lists,
            live_entries,
        ),
    )
    attended_heads = join(attended)
    attended_tok, grad_queries, grad_keys, grad_values = (
        lax.all_to_all(attended_heads, "ctx", split_axis=1, concat_axis=2, tiled=True),
        lax.all_to_all(join(query_grad), "ctx", split_axis=1, concat_axis=2, tiled=True),
        lax.all_to_all(join(key_grad), "ctx", split_axis=1, concat_axis=2, tiled=True),
        lax.all_to_all(join(value_grad), "ctx", split_axis=1, concat_axis=2, tiled=True),
    )
    token_rows = attended_tok[0]
    mixed = jnp.dot(token_rows, full_weight.T, preferred_element_type=jnp.float32)
    mixed = mixed.astype(jnp.bfloat16)[None]
    total_tokens = lax.axis_size("dp") * lax.axis_size("ctx") * cot_rows.shape[0]
    grad_scale = 1.0 / math.sqrt(total_tokens)
    term = lax.dot_general(
        cot_rows, token_rows, (((0,), (0,)), ((), ())), preferred_element_type=jnp.float32
    )
    grad_weight = lax.psum_scatter(
        term * grad_scale, ("dp", "ctx"), scatter_dimension=0, tiled=True
    )
    return (mixed, grad_queries, grad_keys, grad_values, grad_weight)


def solution(mesh):
    return jax.shard_map(
        on_device,
        mesh=mesh,
        in_specs=(
            P("dp", "ctx", None),
            P("dp", "ctx", None),
            P("dp", "ctx", None),
            P(("dp", "ctx"), None),
            P("dp", "ctx", None),
            P("dp", "ctx", None, None),
            P("dp", None),
        ),
        out_specs=(
            P("dp", "ctx", None),
            P("dp", "ctx", None),
            P("dp", "ctx", None),
            P("dp", "ctx", None),
            P(("dp", "ctx"), None),
        ),
        check_vma=False,
    )
```

profile of v0, /device:TPU:0, one launch (start us, length us, event | category | flops | bytes accessed | tf_op | source)
XLA Modules:
  0.0 1172.2 jit_solution(4008736325638047405)
XLA Ops:
  10.8 11.4 reduce
  23.1 5.5 all-to-all-start
  29.4 11.4 reduce.1
  41.8 6.2 all-to-all-start.1
  50.4 11.4 reduce.2
  63.0 5.7 all-to-all-start.2
  68.7 256.5 %all-gather.2.cloned.1.call-done = bf16[2048,2048]{1,0:T(8,128)(2,1)} async-done(((bf16[16,2048]{1,0:T(8,128)(2,1)}), bf16[2048,2048]{1,0:T(8,128)(2,1)}) %all-gather.2.cloned.1.call-update) | async-done | bytes 8388624 | tf_op jit(solution)/shard_map/all_gather | solution.py:93
  325.1 4.6 fusion.33
  330.5 11.4 reduce.3
  342.9 8.5 all-to-all-start.3
  363.1 85.7 %while.16 = (s32[]{:T(128)}, bf16[2,16,64,128]{3,2,1,0:T(8,128)(2,1)}, bf16[2,16,64,128]{3,2,1,0:T(8,128)(2,1)}, bf16[2,16,64,128]{3,2,1,0:T(8,128)(2,1)}, bf16[...) while((s32[]{:T(128)}, ...), condition=%wide.region_7.8_spmd, body=%wide.region_1.7_spmd.sunk | while | flops 824310144 | bytes 95252584 | solution.py:117
  383.6 9.7 scatter_custom_fusion.10
  397.0 9.7 scatter_custom_fusion.11
  424.4 9.7 scatter_custom_fusion.10
  437.8 9.7 scatter_custom_fusion.11
  454.5 15.2 %all_to_all.129 = bf16[8,2,16384]{2,1,0:T(2,128)(2,1)S(1)} all-to-all(bf16[8,2,16384]{2,1,0:T(2,128)(2,1)S(1)} %reshape.178), channel_id=1, replica_groups=mesh['dp'=16,'ctx'=8] {'ctx'}, dimensions={0} | all-to-all | bytes 1048576 | tf_op jit(solution)/shard_map/all_to_all | solution.py:130
  470.7 8.0 multiply_bitcast_fusion.1
  478.7 17.6 %copy.196 = f32[2048,2048]{1,0:T(8,128)} copy(f32[2048,2048]{0,1:T(8,128)} %multiply_bitcast_fusion.1) | data formatting | bytes 33554432
  516.2 4.1 all-to-all-start.5
  526.2 4.5 reduce.6
  532.7 6.0 all-to-all-start.6
  542.6 6.0 all-to-all-done.6
  552.2 7.1 fusion.34
  559.3 605.8 %reduce-scatter.4.cloned.1.call-done = f32[16,2048]{1,0:T(8,128)} async-done(((f32[2048,2048]{1,0:T(8,128)}), f32[16,2048]{1,0:T(8,128)}) %reduce-scatter.4.cloned.1.call-update) | async-done | bytes 131088
  (190 shorter events, 107.0 us)
Async XLA Ops:
  7.2 318.0 %copy-start = (bf16[1,128,2048]{2,1,0:T(8,128)(2,1)S(1)}, bf16[1,128,2048]{2,1,0:T(8,128)(2,1)}, u32[]{:S(2)}) copy-start(bf16[1,128,2048]{2,1,0:T(8,128)(2,1)} %param.13) | copy-start | bytes 1572868
  7.2 21.4 %copy-start.6 = (bf16[1,128,2048]{2,1,0:T(8,128)(2,1)S(1)}, bf16[1,128,2048]{2,1,0:T(8,128)(2,1)}, u32[]{:S(2)}) copy-start(bf16[1,128,2048]{2,1,0:T(8,128)(2,1)} %param.10) | copy-start | bytes 1572868
  7.2 317.9 %all-gather.2.cloned.1.call-start = ((), (), s32[]{:S(2)}) async-start(), calls=%async_computation.9 | async-start | bytes 8454144 | tf_op jit(solution)/shard_map/all_gather | solution.py:93
  23.1 18.6 %all-to-all-start = ((bf16[8,2,16384]{2,1,0:T(2,128)(2,1)}), bf16[8,2,16384]{2,1,0:T(2,128)(2,1)S(1)}, u32[]{:S(2)}, u32[]{:S(2)}) async-start(bf16[8,2,16384]{2,1,0:T(2,128)(2,1)} %reshape.170), calls=%async_computation | async-start | bytes 1048576 | tf_op jit(solution)/shard_map/all_to_all | solution.py:97
  29.4 33.4 %copy-start.15 = (s32[1,2]{1,0:T(1,128)S(1)}, s32[1,2]{1,0:T(1,128)}, u32[]{:S(2)}) copy-start(s32[1,2]{1,0:T(1,128)} %param.15) | copy-start | bytes 28
  29.4 33.5 %copy-start.14 = (s32[1,2,16,3]{2,1,3,0:T(2,128)S(1)}, s32[1,2,16,3]{2,1,3,0:T(2,128)}, u32[]{:S(2)}) copy-start(s32[1,2,16,3]{2,1,3,0:T(2,128)} %param.14) | copy-start | bytes 1156
  41.8 21.2 %all-to-all-start.1 = ((bf16[8,2,16384]{2,1,0:T(2,128)(2,1)}), bf16[8,2,16384]{2,1,0:T(2,128)(2,1)S(1)}, u32[]{:S(2)}, u32[]{:S(2)}) async-start(bf16[8,2,16384]{2,1,0:T(2,128)(2,1)} %reshape.172), calls=%async_computation.1 | async-start | bytes 1048576 | tf_op jit(solution)/shard_map/all_to_all | solution.py:98
  63.0 279.9 %all-to-all-start.2 = ((bf16[8,2,16384]{2,1,0:T(2,128)(2,1)}), bf16[8,2,16384]{2,1,0:T(2,128)(2,1)}, u32[]{:S(2)}, u32[]{:S(2)}) async-start(bf16[8,2,16384]{2,1,0:T(2,128)(2,1)} %reshape.174), calls=%async_computation.2 | async-start | bytes 1048576 | tf_op jit(solution)/shard_map/all_to_all | solution.py:99
  342.9 18.3 %all-to-all-start.3 = ((bf16[8,2,16384]{2,1,0:T(2,128)(2,1)}), bf16[8,2,16384]{2,1,0:T(2,128)(2,1)S(1)}, u32[]{:S(2)}, u32[]{:S(2)}) async-start(bf16[8,2,16384]{2,1,0:T(2,128)(2,1)} %reshape.176), calls=%async_computation.3 | async-start | bytes 1048576 | tf_op jit(solution)/shard_map/all_to_all | solution.py:100
  351.4 813.7 %reduce-scatter.4.cloned.1.call-start = ((), (), s32[]{:S(2)}) async-start(), calls=%async_computation.10 | async-start | bytes 16908288
  372.5 2.2 copy-start.3
  372.5 2.2 copy-start.12
  374.7 2.6 copy-start.5
  383.6 9.8 copy-start.2
  397.0 9.8 copy-start.7
  397.0 9.8 copy-start.10
  413.4 2.2 copy-start.12
  415.6 2.6 copy-start.5
  424.4 9.8 copy-start.2
  437.8 9.8 copy-start.7
  437.8 9.8 copy-start.10
  502.8 13.4 %all-to-all-start.7 = ((bf16[8,2,16384]{2,1,0:T(2,128)(2,1)}), bf16[8,2,16384]{2,1,0:T(2,128)(2,1)S(1)}, u32[]{:S(2)}, u32[]{:S(2)}) async-start(bf16[8,2,16384]{2,1,0:T(2,128)(2,1)} %reshape.184), calls=%async_computation.7 | async-start | bytes 1048576 | tf_op jit(solution)/shard_map/all_to_all | solution.py:133
  516.2 16.5 %all-to-all-start.5 = ((bf16[8,2,16384]{2,1,0:T(2,128)(2,1)}), bf16[8,2,16384]{2,1,0:T(2,128)(2,1)S(1)}, u32[]{:S(2)}, u32[]{:S(2)}) async-start(bf16[8,2,16384]{2,1,0:T(2,128)(2,1)} %reshape.180), calls=%async_computation.5 | async-start | bytes 1048576 | tf_op jit(solution)/shard_map/all_to_all | solution.py:131
  532.7 15.9 %all-to-all-start.6 = ((bf16[8,2,16384]{2,1,0:T(2,128)(2,1)}), bf16[8,2,16384]{2,1,0:T(2,128)(2,1)}, u32[]{:S(2)}, u32[]{:S(2)}) async-start(bf16[8,2,16384]{2,1,0:T(2,128)(2,1)} %reshape.182), calls=%async_computation.6 | async-start | bytes 1048576 | tf_op jit(solution)/shard_map/all_to_all | solution.py:132
  (12 other events, 15.8 us)
Sparse Core Ops, SparseCore 0:
  9.7 315.3 all-gather.1
  496.4 668.5 reduce-scatter.3
where the time goes:
time: 1180 us; the launch traced here: 1170 us
  waiting for transfers between devices  874 us (74%)
  other arithmetic  104 us (9%)
  local copies, waits for them, and re-layouts  75.7 us (6%)
  matrix products  44.2 us (4%)
  starting transfers between devices  40 us (3%)
  blocking collectives  15.2 us (1%)
  between operations  14.7 us (1%)
    unnamed x3, waiting for transfers between devices  606 us
    all_gather x1, waiting for transfers between devices, on_device(): full_weight = lax.all_gather(out_weight, ('dp', 'ctx'), axis=0, tiled=True)  256 us
    unnamed x8, other arithmetic  61.4 us
    unnamed x42, local copies, waits for them, and re-layouts  43.4 us
  transfers between devices with their start and end apart: 9, of which 5 were waited for; matrix products, arithmetic and copies ran while one was open for 9% of the time, Pallas kernels for 0%

commit v1 on v0

--- a/solution.py
+++ b/solution.py
@@ -90,7 +90,10 @@
 
 def on_device(queries, keys, values, out_weight, cotangent, rand_blocks, glob_blocks):
     cot_rows = cotangent[0]
-    full_weight = lax.all_gather(out_weight, ("dp", "ctx"), axis=0, tiled=True)
+    full_weight = jnp.concatenate(
+        lax.all_to_all(jnp.stack([out_weight] * lax.axis_size(("dp", "ctx"))), ("dp", "ctx"), 0, 0),
+        axis=0,
+    )
     head_cot = jnp.dot(cot_rows, full_weight, preferred_element_type=jnp.float32)
     head_cot = head_cot.astype(jnp.bfloat16)[None]
     query_heads, key_heads, value_heads, cot_heads = (

time: 1180 us -> 1030 us (0.87)
  waiting for transfers between devices: 874 us -> 708 us
  blocking collectives: 15.2 us -> 29 us
    all_gather x1 -> x0, waiting for transfers between devices: 256 us -> none  [on_device(): full_weight = lax.all_gather(out_weight, ('dp', 'ctx'), axis=0, tiled=True)]
    all_to_all x1, waiting for transfers between devices: 0.01 us -> 90.3 us  [on_device(): lax.all_to_all(jnp.stack([out_weight] * lax.axis_size(('dp', 'ctx'))), ('...]
    all_to_all x0 -> x1, blocking collectives: none -> 15 us  [on_device(): lax.all_to_all(keys, 'ctx', split_axis=2, concat_axis=1, tiled=True)]
    unnamed x3 -> x2, waiting for transfers between devices: 606 us -> 610 us
    unnamed x42 -> x46, local copies, waits for them, and re-layouts: 43.4 us -> 41.1 us
  transfers between devices with their start and end apart: 9 -> 8, of which waited for: 5 -> 5; matrix products, arithmetic and copies ran while one was open for 9% -> 9% of each run, Pallas kernels for 0% -> 0%
where the time goes in v1:
time: 1030 us; the launch traced here: 1020 us
  waiting for transfers between devices  708 us (69%)
  other arithmetic  104 us (10%)
  local copies, waits for them, and re-layouts  77.7 us (8%)
  matrix products  44.2 us (4%)
  starting transfers between devices  38.2 us (4%)
  blocking collectives  29 us (3%)
  between operations  14.7 us (1%)
    unnamed x2, waiting for transfers between devices  610 us
    all_to_all x1, waiting for transfers between devices, on_device(): lax.all_to_all(jnp.stack([out_weight] * lax.axis_size(('dp', 'ctx'))), ('...  90.3 us
    unnamed x8, other arithmetic  61.5 us
    unnamed x46, local copies, waits for them, and re-layouts  41.1 us
  transfers between devices with their start and end apart: 8, of which 5 were waited for; matrix products, arithmetic and copies ran while one was open for 9% of the time, Pallas kernels for 0%

profile of v1, /device:TPU:0, one launch (start us, length us, event | category | flops | bytes accessed | tf_op | source)
XLA Modules:
  0.0 1021.4 jit_solution(13006633694909111756)
XLA Ops:
  10.1 11.5 %reduce = bf16[2048,128]{1,0:T(8,128)(2,1)S(1)} reduce(bf16[2048,1,128]{2,1,0:T(2,128)(2,1)S(1)} %bitcast.231, bf16[]{:T(256)} %broadcast.91), dimensions={1}, to_apply=%bitcast.132.reduce_sub_computation | reduce | bytes 1048578
  22.5 5.5 all-to-all-start
  28.8 11.4 %reduce.1 = bf16[2048,128]{1,0:T(8,128)(2,1)S(1)} reduce(bf16[2048,1,128]{2,1,0:T(2,128)(2,1)S(1)} %bitcast.237, bf16[]{:T(256)} %broadcast.91), dimensions={1}, to_apply=%bitcast.134.reduce_sub_computation | reduce | bytes 1048578
  40.3 15.0 %all_to_all.134 = bf16[8,2,16384]{2,1,0:T(2,128)(2,1)S(1)} all-to-all(bf16[8,2,16384]{2,1,0:T(2,128)(2,1)S(1)} %reshape.178), channel_id=1, replica_groups=mesh['dp'=16,'ctx'=8] {'ctx'}, dimensions={0} | all-to-all | bytes 1048576 | tf_op jit(solution)/shard_map/all_to_all | solution.py:101
  55.3 4.3 stack.2
  59.6 9.2 all-to-all-start.3
  69.6 11.4 %reduce.2 = bf16[2048,128]{1,0:T(8,128)(2,1)S(1)} reduce(bf16[2048,1,128]{2,1,0:T(2,128)(2,1)S(1)} %bitcast.238, bf16[]{:T(256)} %broadcast.91), dimensions={1}, to_apply=%bitcast.136.reduce_sub_computation | reduce | bytes 1048578
  82.2 90.3 %all-to-all-done.3 = bf16[128,16,2048]{2,1,0:T(8,128)(2,1)} async-done(((bf16[128,16,2048]{2,1,0:T(8,128)(2,1)}), bf16[128,16,2048]{2,1,0:T(8,128)(2,1)}, u32[]{:S(2)}, u32[]{:S(2)}) %all-to-all-start.3) | async-done | bytes 8388640 | tf_op jit(solution)/shard_map/all_to_all | solution.py:94
  176.6 4.6 fusion.33
  182.0 11.4 %reduce.3 = bf16[2048,128]{1,0:T(8,128)(2,1)S(1)} reduce(bf16[2048,1,128]{2,1,0:T(2,128)(2,1)S(1)} %bitcast.233, bf16[]{:T(256)} %broadcast.91), dimensions={1}, to_apply=%bitcast.138.reduce_sub_computation | reduce | bytes 1048578
  194.4 5.6 all-to-all-start.4
  210.2 87.4 %while.16 = (s32[]{:T(128)}, bf16[2,16,64,128]{3,2,1,0:T(8,128)(2,1)}, bf16[2,16,64,128]{3,2,1,0:T(8,128)(2,1)}, bf16[2,16,64,128]{3,2,1,0:T(8,128)(2,1)}, bf16[...) while((s32[]{:T(128)}, ...), condition=%wide.region_7.8_spmd, body=%wide.region_1.7_spmd.sunk | while | flops 824310144 | bytes 95252584 | solution.py:120
  232.1 9.7 scatter_custom_fusion.10
  245.6 9.7 scatter_custom_fusion.11
  273.0 9.7 scatter_custom_fusion.10
  286.4 9.7 scatter_custom_fusion.11
  303.3 14.1 %all_to_all.135 = bf16[8,2,16384]{2,1,0:T(2,128)(2,1)S(1)} all-to-all(bf16[8,2,16384]{2,1,0:T(2,128)(2,1)S(1)} %reshape.184), channel_id=1, replica_groups=mesh['dp'=16,'ctx'=8] {'ctx'}, dimensions={0} | all-to-all | bytes 1048576 | tf_op jit(solution)/shard_map/all_to_all | solution.py:133
  318.3 8.0 multiply_bitcast_fusion.1
  326.4 17.6 %copy.196 = f32[2048,2048]{1,0:T(8,128)} copy(f32[2048,2048]{0,1:T(8,128)} %multiply_bitcast_fusion.1) | data formatting | bytes 33554432
  372.7 4.5 reduce.6
  379.2 6.0 all-to-all-start.7
  389.0 4.7 all-to-all-done.7
  397.4 7.1 fusion.34
  404.5 609.8 %reduce-scatter.4.cloned.1.call-done = f32[16,2048]{1,0:T(8,128)} async-done(((f32[2048,2048]{1,0:T(8,128)}), f32[16,2048]{1,0:T(8,128)}) %reduce-scatter.4.cloned.1.call-update) | async-done | bytes 131088
  (193 shorter events, 109.6 us)
Async XLA Ops:
  7.2 169.5 %copy-start = (bf16[1,128,2048]{2,1,0:T(8,128)(2,1)S(1)}, bf16[1,128,2048]{2,1,0:T(8,128)(2,1)}, u32[]{:S(2)}) copy-start(bf16[1,128,2048]{2,1,0:T(8,128)(2,1)} %param.13) | copy-start | bytes 1572868
  7.2 20.8 %copy-start.6 = (bf16[1,128,2048]{2,1,0:T(8,128)(2,1)S(1)}, bf16[1,128,2048]{2,1,0:T(8,128)(2,1)}, u32[]{:S(2)}) copy-start(bf16[1,128,2048]{2,1,0:T(8,128)(2,1)} %param.10) | copy-start | bytes 1572868
  10.1 45.2 %copy-start.15 = (bf16[16,2048]{1,0:T(8,128)(2,1)S(1)}, bf16[16,2048]{1,0:T(8,128)(2,1)}, u32[]{:S(2)}) copy-start(bf16[16,2048]{1,0:T(8,128)(2,1)} %param.12) | copy-start | bytes 196612
  22.5 17.8 %all-to-all-start = ((bf16[8,2,16384]{2,1,0:T(2,128)(2,1)}), bf16[8,2,16384]{2,1,0:T(2,128)(2,1)S(1)}, u32[]{:S(2)}, u32[]{:S(2)}) async-start(bf16[8,2,16384]{2,1,0:T(2,128)(2,1)} %reshape.176), calls=%async_computation | async-start | bytes 1048576 | tf_op jit(solution)/shard_map/all_to_all | solution.py:100
  59.6 9.2 copy-start.7
  59.6 112.9 %all-to-all-start.3 = ((bf16[128,16,2048]{2,1,0:T(8,128)(2,1)}), bf16[128,16,2048]{2,1,0:T(8,128)(2,1)}, u32[]{:S(2)}, u32[]{:S(2)}) async-start(bf16[128,16,2048]{2,1,0:T(8,128)(2,1)} %stack.2), calls=%async_computation.3 | async-start | bytes 16777216 | tf_op jit(solution)/shard_map/all_to_all | solution.py:94
  68.8 13.2 %copy-start.17 = (s32[1,2]{1,0:T(1,128)S(1)}, s32[1,2]{1,0:T(1,128)}, u32[]{:S(2)}) copy-start(s32[1,2]{1,0:T(1,128)} %param.15) | copy-start | bytes 28
  68.8 13.3 %copy-start.16 = (s32[1,2,16,3]{2,1,3,0:T(2,128)S(1)}, s32[1,2,16,3]{2,1,3,0:T(2,128)}, u32[]{:S(2)}) copy-start(s32[1,2,16,3]{2,1,3,0:T(2,128)} %param.14) | copy-start | bytes 1156
  172.5 21.9 %all-to-all-start.2 = ((bf16[8,2,16384]{2,1,0:T(2,128)(2,1)}), bf16[8,2,16384]{2,1,0:T(2,128)(2,1)}, u32[]{:S(2)}, u32[]{:S(2)}) async-start(bf16[8,2,16384]{2,1,0:T(2,128)(2,1)} %reshape.180), calls=%async_computation.2 | async-start | bytes 1048576 | tf_op jit(solution)/shard_map/all_to_all | solution.py:102
  194.4 13.9 %all-to-all-start.4 = ((bf16[8,2,16384]{2,1,0:T(2,128)(2,1)}), bf16[8,2,16384]{2,1,0:T(2,128)(2,1)S(1)}, u32[]{:S(2)}, u32[]{:S(2)}) async-start(bf16[8,2,16384]{2,1,0:T(2,128)(2,1)} %reshape.182), calls=%async_computation.4 | async-start | bytes 1048576 | tf_op jit(solution)/shard_map/all_to_all | solution.py:103
  200.0 814.3 %reduce-scatter.4.cloned.1.call-start = ((), (), s32[]{:S(2)}) async-start(), calls=%async_computation.10 | async-start | bytes 16908288
  221.1 2.2 copy-start.13
  223.3 2.6 copy-start.5
  232.1 9.8 copy-start.2
  245.6 9.8 copy-start.8
  245.6 9.8 copy-start.11
  261.9 2.2 copy-start.13
  264.1 2.6 copy-start.5
  273.0 9.8 copy-start.2
  286.4 9.8 copy-start.8
  286.4 9.8 copy-start.11
  350.4 12.6 %all-to-all-start.8 = ((bf16[8,2,16384]{2,1,0:T(2,128)(2,1)}), bf16[8,2,16384]{2,1,0:T(2,128)(2,1)S(1)}, u32[]{:S(2)}, u32[]{:S(2)}) async-start(bf16[8,2,16384]{2,1,0:T(2,128)(2,1)} %reshape.190), calls=%async_computation.8 | async-start | bytes 1048576 | tf_op jit(solution)/shard_map/all_to_all | solution.py:136
  363.1 16.1 %all-to-all-start.6 = ((bf16[8,2,16384]{2,1,0:T(2,128)(2,1)}), bf16[8,2,16384]{2,1,0:T(2,128)(2,1)S(1)}, u32[]{:S(2)}, u32[]{:S(2)}) async-start(bf16[8,2,16384]{2,1,0:T(2,128)(2,1)} %reshape.186), calls=%async_computation.6 | async-start | bytes 1048576 | tf_op jit(solution)/shard_map/all_to_all | solution.py:134
  379.2 14.6 %all-to-all-start.7 = ((bf16[8,2,16384]{2,1,0:T(2,128)(2,1)}), bf16[8,2,16384]{2,1,0:T(2,128)(2,1)}, u32[]{:S(2)}, u32[]{:S(2)}) async-start(bf16[8,2,16384]{2,1,0:T(2,128)(2,1)} %reshape.188), calls=%async_computation.7 | async-start | bytes 1048576 | tf_op jit(solution)/shard_map/all_to_all | solution.py:135
  (13 other events, 18.0 us)
Sparse Core Ops, SparseCore 0:
  344.1 670.1 reduce-scatter.3
